TPU v7x, 32 devices: a whole 2x2x4 slice. The times are simulated.
32 devices in a mesh: snap: 2 (over y), gx: 8 (over z, x), gy: 2 (over core).
Axes of the slice: x: 2, y: 2, z: 4, core: 2. Of those that a mesh axis runs over, the one named last changes fastest.
Arguments:
- snapshot: float32 [32, 256, 12, 128], P(('snap', 'gx'), 'gy'), parts along dimension 0, may hold values from -64 to 64
- factor_x: float32 [16, 64], P('gx')
- factor_y: float32 [256, 64], P(None, 'gy')
- factor_var: float32 [12, 4], replicated
Outputs:
- gram: float32 [256, 128], P('snap'), parts along dimension 0
There are 2 independent parts, one for each index of `snap`. A program takes and returns all parts, laid end to end along the dimension named above; an argument that names none is the same for every part. Nothing has to cross between parts.
All inputs are finite; a program needn't handle non-finite values.
Results may differ from a plain program's by a relative error of at most 0.000087.
Values sent between devices are 32-bit elements; how exact they have to be, the bound alone decides.
A program may use at most 64 MiB of HBM per device.

v0:
```python
import jax
import jax.numpy as jnp
from jax import lax
from jax.sharding import PartitionSpec as P

RX = 64
RY = 64
RV = 4


def local(snapshot, factor_x, factor_y, factor_var):
    highest = lax.Precision.HIGHEST
    reduced = jnp.einsum("xyvz,vq->xyqz", snapshot, factor_var, precision=highest)
    local_x = snapshot.shape[0]
    depth = snapshot.shape[3]
    contracted = jnp.einsum(
        "xyqz,yp->xpqz",
        lax.all_gather(reduced, "gy", axis=1, tiled=True),
        factor_y,
        precision=highest,
    )
    all_factor = lax.all_gather(factor_x, "gx", axis=0, tiled=True)
    flattened = contracted.reshape(local_x, -1, depth)
    projected = jnp.einsum(
        "xkz,xr->krz",
        lax.all_to_all(flattened, "gx", split_axis=1, concat_axis=0, tiled=True),
        all_factor,
        precision=highest,
    )
    unfolded = projected.reshape(-1, depth)
    gram_part = jnp.dot(unfolded.T, unfolded, precision=highest, preferred_element_type=jnp.float32)
    summed = lax.psum(gram_part, ("gx", "gy"))
    return summed * (1.0 / (RX * RY * RV))


def solution(mesh):
    in_specs = (P(("snap", "gx"), "gy", None, None), P("gx", None), P(None, "gy"), P())
    out_specs = P("snap", None)
    return jax.shard_map(local, mesh=mesh, in_specs=in_specs, out_specs=out_specs, check_vma=False)
```

profile of v0, /device:TPU:0, one launch (start us, length us, event | category | flops | bytes accessed | tf_op | source)
XLA Modules:
  0.0 145.5 jit_solution(10382246471291874001)
XLA Ops:
  6.5 0.0 copy-start
  6.5 0.0 copy-start.1
  6.5 0.0 all-gather.3.cloned.1.call-start
  6.5 1.4 copy-done
  7.9 3.6 %fusion.2 = f32[2,128,4,128]{3,2,1,0:T(4,128)} fusion(f32[2,128,12,128]{3,1,2,0:T(8,128)S(1)} %copy-done, f32[12,4]{0,1:T(4,128)} %param.7), kind=kOutput, calls=%fused_computation.3 | convolution fusion | flops 18874368 | bytes 2097344 | tf_op jit(solution)/shard_map/xyvz,vq->xyqz/dot_general | solution.py:13
  11.5 0.0 copy-start.2
  11.5 0.0 all-gather.3.cloned.1.call-update
  11.5 11.9 %all-gather.3.cloned.1.call-done = f32[2,256,4,128]{3,2,1,0:T(4,128)} async-done(((f32[2,128,4,128]{3,2,1,0:T(4,128)}), f32[2,256,4,128]{3,2,1,0:T(4,128)}) %all-gather.3.cloned.1.call-update) | async-done | bytes 1048592 | tf_op jit(solution)/shard_map/all_gather | solution.py:18
  23.4 0.0 copy-done.1
  23.4 2.0 %convolution_bitcast_fusion.1 = f32[2,32,4,128]{3,1,2,0:T(8,128)S(1)} fusion(f32[2,256,4,128]{3,2,1,0:T(4,128)} %all-gather.3.cloned.1.call-done, f32[256,32]{0,1:T(8,128)S(1)} %copy-done.1), kind=kOutput, calls=%fused_computation.4 | convolution fusion | flops 100663296 | bytes 1212416 | tf_op jit(solution)/shard_map/xyqz,yp->xpqz/dot_general | solution.py:16
  25.4 0.1 copy.14
  25.5 0.8 copy.15
  26.2 5.8 %all-to-all-start = ((f32[2,128,128]{2,0,1:T(2,128)}), f32[2,128,128]{2,0,1:T(2,128)S(1)}, u32[]{:S(2)}, u32[]{:S(2)}) async-start(f32[2,128,128]{2,0,1:T(2,128)} %copy.15), calls=%async_computation | async-start | bytes 262144 | tf_op jit(solution)/shard_map/all_to_all | solution.py:26
  32.0 0.0 all-reduce.2.cloned.1.call-start
  32.0 0.0 copy-done.2
  32.1 20.9 %all-gather = f32[8,2,64]{2,1,0:T(2,128)S(1)} all-gather(f32[1,2,64]{2,1,0:T(2,128)S(1)} %bitcast.34), channel_id=1, replica_groups=mesh['snap'=2,'gx'=8,'gy'=2] {'gx'}, dimensions={0}, use_global_device_ids=true | all-gather | bytes 4608 | tf_op jit(solution)/shard_map/all_gather | solution.py:22
  53.0 0.0 all-to-all-done
  53.0 0.6 convolution_bitcast_fusion
  53.6 1.7 %convolution_bitcast_fusion.2 = f32[128,128]{1,0:T(8,128)} fusion(f32[16,64,128]{2,1,0:T(8,128)S(1)} %convolution_bitcast_fusion), kind=kOutput, calls=%fused_computation.5 | convolution fusion | flops 201326592 | bytes 589824 | tf_op jit(solution)/shard_map/dot_general | solution.py:31
  55.3 0.0 all-reduce.2.cloned.1.call-update
  55.3 81.9 %all-reduce.2.cloned.1.call-done = f32[128,128]{1,0:T(8,128)} async-done(((f32[128,128]{1,0:T(8,128)}), f32[128,128]{1,0:T(8,128)}) %all-reduce.2.cloned.1.call-update) | async-done | bytes 65552 | tf_op jit(solution)/shard_map/psum | solution.py:32
  137.2 1.5 %broadcast_multiply_fusion = f32[128,128]{1,0:T(8,128)} fusion(f32[128,128]{1,0:T(8,128)} %all-reduce.2.cloned.1.call-done), kind=kLoop, calls=%fused_computation.9 | loop fusion | flops 16384 | bytes 131072 | tf_op jit(solution)/shard_map/mul | solution.py:33
  (2 shorter events, 0.0 us)
Async XLA Ops:
  6.5 1.4 copy-start
  6.5 16.9 %copy-start.1 = (f32[256,32]{0,1:T(8,128)S(1)}, f32[256,32]{0,1:T(8,128)}, u32[]{:S(2)}) copy-start(f32[256,32]{0,1:T(8,128)} %param.6) | copy-start | bytes 98308
  6.5 16.9 %all-gather.3.cloned.1.call-start = ((), (), s32[]{:S(2)}) async-start(), calls=%async_computation.1 | async-start | bytes 1572864 | tf_op jit(solution)/shard_map/all_gather | solution.py:18
  11.5 20.5 %copy-start.2 = (f32[2,64]{1,0:T(2,128)S(1)}, f32[2,64]{1,0:T(2,128)}, u32[]{:S(2)}) copy-start(f32[2,64]{1,0:T(2,128)} %param.5) | copy-start | bytes 1540
  26.2 26.8 %all-to-all-start = ((f32[2,128,128]{2,0,1:T(2,128)}), f32[2,128,128]{2,0,1:T(2,128)S(1)}, u32[]{:S(2)}, u32[]{:S(2)}) async-start(f32[2,128,128]{2,0,1:T(2,128)} %copy.15), calls=%async_computation | async-start | bytes 262144 | tf_op jit(solution)/shard_map/all_to_all | solution.py:26
  32.0 105.2 %all-reduce.2.cloned.1.call-start = ((), (), s32[]{:S(2)}) async-start(), calls=%async_computation.2 | async-start | bytes 131072 | tf_op jit(solution)/shard_map/psum | solution.py:32
Sparse Core Ops, SparseCore 0:
  11.6 11.7 all-gather.2
  55.5 81.7 all-reduce.1
where the time goes:
time: 147 us; the launch traced here: 146 us
  waiting for transfers between devices  93.8 us (64%)
  blocking collectives  20.9 us (14%)
  between operations  13.4 us (9%)
  matrix products  7.79 us (5%)
  starting transfers between devices  5.8 us (4%)
  local copies, waits for them, and re-layouts  2.27 us (2%)
  other arithmetic  1.47 us (1%)
    psum x1, waiting for transfers between devices, local(): summed = lax.psum(gram_part, ('gx', 'gy'))  81.9 us
    all_gather x1, blocking collectives, local(): all_factor = lax.all_gather(factor_x, 'gx', axis=0, tiled=True)  20.9 us
    all_gather x1, waiting for transfers between devices, local(): lax.all_gather(reduced, 'gy', axis=1, tiled=True)  11.9 us
    all_to_all x1, starting transfers between devices, local(): lax.all_to_all(flattened, 'gx', split_axis=1, concat_axis=0, tiled=True)  5.76 us
    dot_general x1, matrix products, local(): jnp.einsum('xyvz,vq->xyqz', snapshot, factor_var, precision=highest)  3.55 us
  transfers between devices with their start and end apart: 3, of which 2 were waited for; matrix products, arithmetic and copies ran while one was open for 0% of the time, Pallas kernels for 0%

commit v1 on v0

v1 whole, which is shorter than its diff:
```python
import functools

import jax
import jax.numpy as jnp
from jax import lax
from jax.experimental import pallas as pl
from jax.experimental.pallas import tpu as pltpu
from jax.sharding import PartitionSpec as P

MESH = pl.DeviceIdType.MESH
HIGHEST = lax.Precision.HIGHEST
CORES = 2
SUBLANES = 8


def dot(a, b, dims=((1,), (0,))):
    return lax.dot_general(a, b, (dims, ((), ())), precision=HIGHEST, preferred_element_type=jnp.float32)


def loop(first, last, body):
    def step(i, carry):
        body(i)
        return carry

    lax.fori_loop(first, last, step, 0, unroll=(last - first) <= 16)


def kernel(
    n_gx, scale,
    snap_ref, fx_ref, fyt_ref, fv_ref, out_ref,
    snap, reduced, fx_all, fy_send, fy_recv, half_send, half_recv, part, blocks, gram, pieces,
    snap_sem, fy_sems, fx_send, fx_recv, half_ssem, half_rsem, a2a_send, a2a_recv, rs_send, rs_recv, ag_send, ag_recv,
):
    gx, gy = lax.axis_index("gx"), lax.axis_index("gy")
    other = 1 - gy
    total = n_gx * CORES
    me = gx * CORES + gy
    local_x, n_var, local_y, depth = snap.shape
    n_q = reduced.shape[0]
    _, _, k, _ = blocks.shape
    per_q = n_gx // n_q
    owners = min(total, depth // SUBLANES)

    def device(t):
        return {"gx": t // CORES, "gy": t % CORES}

    def remote(src, dst, send, recv, where):
        return pltpu.make_async_remote_copy(
            src_ref=src, dst_ref=dst, send_sem=send, recv_sem=recv, device_id=where, device_id_type=MESH
        )

    loads = [pltpu.make_async_copy(snap_ref.at[x], snap.at[x], snap_sem.at[x]) for x in range(local_x)]
    for load in loads:
        load.start()

    barrier = pltpu.get_barrier_semaphore()
    loop(1, total, lambda s: pl.semaphore_signal(
        barrier, inc=1, device_id=device(lax.rem(me + s, total)), device_id_type=MESH))

    fx = fx_ref[...]
    rank = fx.shape[1]
    fx_wide = jnp.concatenate([fx, jnp.zeros((local_x, depth - rank), jnp.float32)], axis=1) if rank < depth else fx
    for x in range(local_x):
        fx_all[gx, x] = fx_wide[x : x + 1]
    fy_send[...] = fyt_ref[:, pl.ds(pl.multiple_of(other * local_y, local_y), local_y)]
    fy_mine = fyt_ref[:, pl.ds(pl.multiple_of(gy * local_y, local_y), local_y)]

    pl.semaphore_wait(barrier, total - 1)

    fy_copy = remote(fy_send, fy_recv, fy_sems.at[0], fy_sems.at[1], {"gy": other})
    fy_copy.start()

    def fx_copy(j):
        return remote(fx_all.at[gx], fx_all.at[gx], fx_send.at[j], fx_recv.at[gx], {"gx": j})

    loop(1, n_gx, lambda s: fx_copy(lax.rem(gx + s, n_gx)).start())

    rows = 16
    for x in range(local_x):
        loads[x].wait()

        def var_step(i, carry, x=x):
            at = pl.ds(pl.multiple_of(i * rows, rows), rows)
            sums = [None] * n_q
            for v in range(n_var):
                cells = snap[x, v, at, :]
                for q in range(n_q):
                    term = cells * fv_ref[v, q]
                    sums[q] = term if v == 0 else sums[q] + term
            for q in range(n_q):
                reduced[q, at, x * depth : (x + 1) * depth] = sums[q]
            return carry

        lax.fori_loop(0, local_y // rows, var_step, 0)

    def put(ref, q, value):
        for x in range(local_x):
            cells = value[:, x * depth : (x + 1) * depth]
            ref[q * per_q : (q + 1) * per_q, x] = cells.reshape(per_q, k, depth)

    fy_copy.wait_recv()
    fy_theirs = fy_recv[...]
    halves = []
    for q in range(n_q):
        put(half_send, q, dot(fy_theirs, reduced[q]))
        at = pl.ds(q * per_q, per_q)
        half = remote(half_send.at[at], half_recv.at[at], half_ssem.at[q], half_rsem.at[q], {"gy": other})
        half.start()
        halves.append(half)
    for q in range(n_q):
        put(part, q, dot(fy_mine, reduced[q]))

    def block_copy(j):
        return remote(part.at[j], blocks.at[gx], a2a_send.at[j], a2a_recv.at[gx], {"gx": j})

    for q in range(n_q):
        at = pl.ds(q * per_q, per_q)
        halves[q].wait_recv()
        part[at] = part[at] + half_recv[at]

        def send_block(j):
            @pl.when(j != gx)
            def _():
                block_copy(j).start()

        loop(q * per_q, (q + 1) * per_q, send_block)
    blocks[gx] = part[gx]

    def arrived(sems, ref, j):
        remote(ref.at[gx], ref.at[j], fx_send.at[j], sems.at[j], {"gx": j}).wait_recv()

    loop(1, n_gx, lambda s: arrived(fx_recv, fx_all, lax.rem(gx + s, n_gx)))
    wide = n_gx * local_x * k
    factor = jnp.broadcast_to(fx_all[...], (n_gx, local_x, k, depth)).reshape(wide, depth)
    largest = jnp.max(jnp.abs(factor), axis=1, keepdims=True)
    largest = jnp.where(largest > 0.0, largest, 1.0)
    unit = factor / largest
    same = (
        lax.broadcasted_iota(jnp.int32, (wide, wide), 0) % k
        == lax.broadcasted_iota(jnp.int32, (wide, wide), 1) % k
    )
    mixing = jnp.where(same, dot(unit, unit, ((1,), (1,))), 0.0)

    loop(1, n_gx, lambda s: arrived(a2a_recv, blocks, lax.rem(gx + s, n_gx)))
    cells = blocks[...].reshape(wide, depth) * largest
    gram[...] = dot(cells, dot(mixing, cells), ((0,), (0,)))

    def piece_copy(t):
        at = pl.ds(pl.multiple_of(t * SUBLANES, SUBLANES), SUBLANES)
        return remote(gram.at[at], pieces.at[me], rs_send.at[t], rs_recv.at[me], device(t))

    def row_copy(t):
        at = pl.ds(pl.multiple_of(me * SUBLANES, SUBLANES), SUBLANES)
        return remote(out_ref.at[at], out_ref.at[at], ag_send.at[t], ag_recv.at[me], device(t))

    def owned(t, body):
        if owners == total:
            body()
        else:
            pl.when(t < owners)(body)

    def others(body):
        loop(1, total, lambda s: body(lax.rem(me + s, total)))

    others(lambda t: owned(t, lambda: piece_copy(t).start()))

    def finish():
        at = pl.ds(pl.multiple_of(me * SUBLANES, SUBLANES), SUBLANES)
        pieces[me] = gram[at]
        others(lambda t: remote(gram.at[at], pieces.at[t], rs_send.at[t], rs_recv.at[t], device(t)).wait_recv())
        out_ref[at] = jnp.sum(pieces[...], axis=0) * scale
        others(lambda t: row_copy(t).start())

    owned(me, finish)

    def row_arrived(t):
        at = pl.ds(pl.multiple_of(t * SUBLANES, SUBLANES), SUBLANES)
        remote(out_ref.at[at], out_ref.at[at], ag_send.at[t], ag_recv.at[t], device(t)).wait_recv()

    others(lambda t: owned(t, lambda: row_arrived(t)))

    fy_copy.wait_send()
    for half in halves:
        half.wait_send()

    def sent(j):
        fx_copy(j).wait_send()
        block_copy(j).wait_send()

    loop(1, n_gx, lambda s: sent(lax.rem(gx + s, n_gx)))
    others(lambda t: owned(t, lambda: piece_copy(t).wait_send()))
    owned(me, lambda: others(lambda t: row_copy(t).wait_send()))


def solution(mesh):
    n_gx = mesh.shape["gx"]
    assert mesh.shape["gy"] == CORES

    def local(snapshot, factor_x, factor_y, factor_var):
        local_x, local_y, n_var, depth = snapshot.shape
        n_q = factor_var.shape[1]
        half_p = factor_y.shape[1]
        rank = factor_x.shape[1]
        k = half_p * n_q // n_gx
        total = n_gx * CORES
        scale = 1.0 / (rank * half_p * CORES * n_q)
        f32 = jnp.float32
        block = (n_gx, local_x, k, depth)
        dma = pltpu.SemaphoreType.DMA
        return pl.pallas_call(
            functools.partial(kernel, n_gx, scale),
            out_shape=jax.ShapeDtypeStruct((depth, depth), f32),
            in_specs=[
                pl.BlockSpec(memory_space=pl.ANY),
                pl.BlockSpec(memory_space=pltpu.VMEM),
                pl.BlockSpec(memory_space=pltpu.VMEM),
                pl.BlockSpec(memory_space=pltpu.SMEM),
            ],
            out_specs=pl.BlockSpec(memory_space=pltpu.VMEM),
            scratch_shapes=[
                pltpu.VMEM((local_x, n_var, local_y, depth), f32),
                pltpu.VMEM((n_q, local_y, local_x * depth), f32),
                pltpu.VMEM((n_gx, local_x, 1, depth), f32),
                pltpu.VMEM((half_p, local_y), f32),
                pltpu.VMEM((half_p, local_y), f32),
                pltpu.VMEM(block, f32),
                pltpu.VMEM(block, f32),
                pltpu.VMEM(block, f32),
                pltpu.VMEM(block, f32),
                pltpu.VMEM((depth, depth), f32),
                pltpu.VMEM((total, SUBLANES, depth), f32),
                dma((local_x,)), dma((2,)),
                dma((n_gx,)), dma((n_gx,)),
                dma((n_q,)), dma((n_q,)),
                dma((n_gx,)), dma((n_gx,)),
                dma((total,)), dma((total,)),
                dma((total,)), dma((total,)),
            ],
            compiler_params=pltpu.CompilerParams(
                collective_id=0, has_side_effects=True, vmem_limit_bytes=24 * 1024 * 1024
            ),
        )(jnp.transpose(snapshot, (0, 2, 1, 3)), factor_x, factor_y.T, factor_var)

    in_specs = (P(("snap", "gx"), "gy", None, None), P("gx", None), P(None, "gy"), P())
    return jax.shard_map(local, mesh=mesh, in_specs=in_specs, out_specs=P("snap", None), check_vma=False)
```

time: 147 us -> 27.8 us (0.19)
  waiting for transfers between devices: 93.8 us -> 0 us
  Pallas kernels: 0 us -> 23.3 us
  blocking collectives: 20.9 us -> 0 us
  between operations: 13.4 us -> 0.01 us
  matrix products: 7.79 us -> 0 us
  starting transfers between devices: 5.8 us -> 0 us
  local copies, waits for them, and re-layouts: 2.27 us -> 4.24 us
  other arithmetic: 1.47 us -> 0 us
    psum x1 -> x0, waiting for transfers between devices: 81.9 us -> none  [local(): summed = lax.psum(gram_part, ('gx', 'gy'))]
    pallas_call x0 -> x1, Pallas kernels: none -> 23.3 us  [local(): pl.pallas_call(functools.partial(kernel, n_gx, scale), out_shape=jax.Shap...]
    all_gather x1 -> x0, blocking collectives: 20.9 us -> none  [local(): all_factor = lax.all_gather(factor_x, 'gx', axis=0, tiled=True)]
    all_gather x1 -> x0, waiting for transfers between devices: 11.9 us -> none  [local(): lax.all_gather(reduced, 'gy', axis=1, tiled=True)]
    dot_general x4 -> x0, matrix products: 7.79 us -> none  [the longest x1 3.55 us: local(): jnp.einsum('xyvz,vq->xyqz', snapshot, factor_var, precision=highest)]
    all_to_all x1 -> x0, starting transfers between devices: 5.76 us -> none  [local(): lax.all_to_all(flattened, 'gx', split_axis=1, concat_axis=0, tiled=True)]
    unnamed x6 -> x8, local copies, waits for them, and re-layouts: 1.41 us -> 4.24 us
    mul x1 -> x0, other arithmetic: 1.47 us -> none  [local(): return summed * (1.0 / (RX * RY * RV))]
  transfers between devices with their start and end apart: 3 -> 0, of which waited for: 2 -> 0; matrix products, arithmetic and copies ran while one was open for 0% -> 0% of each run, Pallas kernels for 0% -> 0%
where the time goes in v1:
time: 27.8 us; the launch traced here: 27.6 us
  Pallas kernels  23.3 us (84%)
  local copies, waits for them, and re-layouts  4.24 us (15%)
    pallas_call x1, Pallas kernels, local(): pl.pallas_call(functools.partial(kernel, n_gx, scale), out_shape=jax.Shap...  23.3 us
    unnamed x8, local copies, waits for them, and re-layouts  4.24 us

profile of v1, /device:TPU:0, one launch (start us, length us, event | category | flops | bytes accessed | tf_op | source)
XLA Modules:
  0.0 27.6 jit_solution(4855650626208615885)
XLA Ops:
  0.0 0.8 %copy.5.fv_ref = f32[12,4]{1,0:T(8,128)S(1)} copy(f32[12,4]{0,1:T(4,128)} %param.7) | data formatting | bytes 384 | tf_op args[3]
  0.8 0.0 copy-start
  0.8 1.4 %copy-done = f32[2,128,12,128]{3,1,2,0:T(8,128)S(1)} copy-done((f32[2,128,12,128]{3,1,2,0:T(8,128)S(1)}, f32[2,128,12,128]{3,1,2,0:T(8,128)}, u32[]{:S(2)}) %copy-start) | copy-done | bytes 1572888
  2.2 0.0 copy-start.1
  2.2 0.8 %copy-done.1 = f32[256,32]{0,1:T(8,128)S(1)} copy-done((f32[256,32]{0,1:T(8,128)S(1)}, f32[256,32]{0,1:T(8,128)}, u32[]{:S(2)}) %copy-start.1) | copy-done | bytes 32792
  2.9 0.0 copy-start.2
  2.9 0.7 %copy-done.2 = f32[2,64]{1,0:T(2,128)S(1)} copy-done((f32[2,64]{1,0:T(2,128)S(1)}, f32[2,64]{1,0:T(2,128)}, u32[]{:S(2)}) %copy-start.2) | copy-done | bytes 536
  3.6 23.3 %shard_map.46 = f32[128,128]{1,0:T(8,128)S(1)} custom-call(f32[2,12,128,128]{3,2,1,0:T(8,128)S(1)} %bitcast.2, f32[2,64]{1,0:T(2,128)S(1)} %copy-done.2, f32[32,256]{1,0:T(8,128)S(1)} %bitcast.3, f32[12,4]{1,0:T(8,128)S(1)} %copy.5.fv_ref), custom_call_target="tpu_custom_call" | custom-call | tf_op jit(solution)/shard_map/pallas_call | solution.py:210
  26.9 0.6 %copy.7 = f32[128,128]{1,0:T(8,128)} copy(f32[128,128]{1,0:T(8,128)S(1)} %shard_map.46) | data formatting | bytes 131072
Async XLA Ops:
  0.8 1.4 %copy-start = (f32[2,128,12,128]{3,1,2,0:T(8,128)S(1)}, f32[2,128,12,128]{3,1,2,0:T(8,128)}, u32[]{:S(2)}) copy-start(f32[2,128,12,128]{3,1,2,0:T(8,128)} %param.4) | copy-start | bytes 4718596
  2.2 0.8 %copy-start.1 = (f32[256,32]{0,1:T(8,128)S(1)}, f32[256,32]{0,1:T(8,128)}, u32[]{:S(2)}) copy-start(f32[256,32]{0,1:T(8,128)} %param.6) | copy-start | bytes 98308
  2.9 0.7 %copy-start.2 = (f32[2,64]{1,0:T(2,128)S(1)}, f32[2,64]{1,0:T(2,128)}, u32[]{:S(2)}) copy-start(f32[2,64]{1,0:T(2,128)} %fx_ref.1) | copy-start | bytes 1540

commit v2 on v1

v2 whole, which is shorter than its diff:
```python
import functools

import jax
import jax.numpy as jnp
from jax import lax
from jax.experimental import pallas as pl
from jax.experimental.pallas import tpu as pltpu
from jax.sharding import PartitionSpec as P

MESH = pl.DeviceIdType.MESH
HIGHEST = lax.Precision.HIGHEST
CORES = 2
CHUNKS = 4


def dot(a, b, dims=((1,), (0,))):
    return lax.dot_general(a, b, (dims, ((), ())), precision=HIGHEST, preferred_element_type=jnp.float32)


def loop(first, last, body):
    def step(i, carry):
        body(i)
        return carry

    lax.fori_loop(first, last, step, 0, unroll=(last - first) <= 16)


def kernel(
    n_gx, scale,
    snap_in, fx_in, fyt_in, fv_in, out_ref,
    fx_ref, fyt_ref, fv_ref, snap, reduced, fx_all, fy_send, fy_recv, half_send, half_recv, part, blocks, gram, gram_recv, pieces,
    in_sems, snap_sem, fy_sems, fx_send, fx_recv, half_ssem, half_rsem, a2a_send, a2a_recv, rs_send, rs_recv, core_sems,
):
    gx, gy = lax.axis_index("gx"), lax.axis_index("gy")
    other = 1 - gy
    local_x, n_var, local_y, depth = snap.shape
    n_q = reduced.shape[0]
    _, _, k, _ = blocks.shape
    per_q = n_gx // n_q
    half_rows = depth // CORES

    def remote(src, dst, send, recv, where):
        return pltpu.make_async_remote_copy(
            src_ref=src, dst_ref=dst, send_sem=send, recv_sem=recv, device_id=where, device_id_type=MESH
        )

    small = [
        pltpu.make_async_copy(src, dst, in_sems.at[i])
        for i, (src, dst) in enumerate(((fyt_in, fyt_ref), (fx_in, fx_ref), (fv_in, fv_ref)))
    ]
    for load in small:
        load.start()
    chunk = local_y // CHUNKS
    loads = []
    for x in range(local_x):
        for i in range(CHUNKS):
            at = pl.ds(i * chunk, chunk)
            loads.append(pltpu.make_async_copy(snap_in.at[x, :, at], snap.at[x, :, at], snap_sem.at[x * CHUNKS + i]))
    for load in loads:
        load.start()

    barrier = pltpu.get_barrier_semaphore()
    pl.semaphore_signal(barrier, inc=1, device_id={"gy": other}, device_id_type=MESH)
    loop(1, n_gx, lambda s: pl.semaphore_signal(
        barrier, inc=1, device_id={"gx": lax.rem(gx + s, n_gx)}, device_id_type=MESH))

    for load in small:
        load.wait()
    fx = fx_ref[...]
    rank = fx.shape[1]
    fx_wide = jnp.concatenate([fx, jnp.zeros((local_x, depth - rank), jnp.float32)], axis=1) if rank < depth else fx
    for x in range(local_x):
        fx_all[gx, x] = fx_wide[x : x + 1]
    fy_send[...] = fyt_ref[:, pl.ds(pl.multiple_of(other * local_y, local_y), local_y)]
    fy_mine = fyt_ref[:, pl.ds(pl.multiple_of(gy * local_y, local_y), local_y)]

    pl.semaphore_wait(barrier, n_gx)

    fy_copy = remote(fy_send, fy_recv, fy_sems.at[0], fy_sems.at[1], {"gy": other})
    fy_copy.start()

    def fx_copy(j):
        return remote(fx_all.at[gx], fx_all.at[gx], fx_send.at[j], fx_recv.at[gx], {"gx": j})

    loop(1, n_gx, lambda s: fx_copy(lax.rem(gx + s, n_gx)).start())

    rows = 16
    for part_of, load in enumerate(loads):
        x, first = part_of // CHUNKS, part_of % CHUNKS * chunk
        load.wait()

        def var_step(i, carry, x=x, first=first):
            at = pl.ds(pl.multiple_of(first + i * rows, rows), rows)
            sums = [None] * n_q
            for v in range(n_var):
                cells = snap[x, v, at, :]
                for q in range(n_q):
                    term = cells * fv_ref[q, v]
                    sums[q] = term if v == 0 else sums[q] + term
            for q in range(n_q):
                reduced[q, at, x * depth : (x + 1) * depth] = sums[q]
            return carry

        lax.fori_loop(0, chunk // rows, var_step, 0)

    def put(ref, q, value):
        for x in range(local_x):
            cells = value[:, x * depth : (x + 1) * depth]
            ref[q * per_q : (q + 1) * per_q, x] = cells.reshape(per_q, k, depth)

    fy_copy.wait_recv()
    fy_theirs = fy_recv[...]
    halves = []
    for q in range(n_q):
        put(half_send, q, dot(fy_theirs, reduced[q]))
        at = pl.ds(q * per_q, per_q)
        exchange = remote(half_send.at[at], half_recv.at[at], half_ssem.at[q], half_rsem.at[q], {"gy": other})
        exchange.start()
        halves.append(exchange)
    for q in range(n_q):
        put(part, q, dot(fy_mine, reduced[q]))

    def block_copy(j):
        return remote(part.at[j], blocks.at[gx], a2a_send.at[j], a2a_recv.at[gx], {"gx": j})

    for q in range(n_q):
        at = pl.ds(q * per_q, per_q)
        halves[q].wait_recv()
        part[at] = part[at] + half_recv[at]

        def send_block(j):
            @pl.when(j != gx)
            def _():
                block_copy(j).start()

        loop(q * per_q, (q + 1) * per_q, send_block)
    blocks[gx] = part[gx]

    def arrived(sems, ref, j):
        remote(ref.at[gx], ref.at[j], fx_send.at[j], sems.at[j], {"gx": j}).wait_recv()

    loop(1, n_gx, lambda s: arrived(fx_recv, fx_all, lax.rem(gx + s, n_gx)))
    wide = n_gx * local_x * k
    factor = jnp.broadcast_to(fx_all[...], (n_gx, local_x, k, depth)).reshape(wide, depth)
    largest = jnp.max(jnp.abs(factor), axis=1, keepdims=True)
    largest = jnp.where(largest > 0.0, largest, 1.0)
    unit = factor / largest
    same = (
        lax.broadcasted_iota(jnp.int32, (wide, wide), 0) % k
        == lax.broadcasted_iota(jnp.int32, (wide, wide), 1) % k
    )
    mixing = jnp.where(same, dot(unit, unit, ((1,), (1,))), 0.0)

    loop(1, n_gx, lambda s: arrived(a2a_recv, blocks, lax.rem(gx + s, n_gx)))
    cells = blocks[...].reshape(wide, depth) * largest
    gram[...] = dot(cells, dot(mixing, cells), ((0,), (0,)))

    def others(body):
        loop(1, n_gx, lambda s: body(lax.rem(gx + s, n_gx)))

    my_rows = pl.ds(pl.multiple_of(gy * half_rows, half_rows), half_rows)
    other_rows = pl.ds(pl.multiple_of(other * half_rows, half_rows), half_rows)
    gram_copy = remote(gram.at[other_rows], gram_recv, core_sems.at[0], core_sems.at[1], {"gy": other})
    gram_copy.start()
    gram_copy.wait_recv()
    pieces[gx] = gram[my_rows] + gram_recv[...]

    def piece_copy(t):
        return remote(pieces.at[gx], pieces.at[gx], rs_send.at[t], rs_recv.at[gx], {"gx": t})

    others(lambda t: piece_copy(t).start())
    others(lambda t: remote(pieces.at[gx], pieces.at[t], rs_send.at[t], rs_recv.at[t], {"gx": t}).wait_recv())
    out_ref[my_rows] = jnp.sum(pieces[...], axis=0) * scale
    out_copy = remote(out_ref.at[my_rows], out_ref.at[my_rows], core_sems.at[2], core_sems.at[3], {"gy": other})
    out_copy.start()

    fy_copy.wait_send()
    for exchange in halves:
        exchange.wait_send()

    def sent(j):
        fx_copy(j).wait_send()
        block_copy(j).wait_send()

    loop(1, n_gx, lambda s: sent(lax.rem(gx + s, n_gx)))
    others(lambda t: piece_copy(t).wait_send())
    gram_copy.wait_send()
    out_copy.wait_send()
    remote(out_ref.at[my_rows], out_ref.at[other_rows], core_sems.at[2], core_sems.at[3], {"gy": other}).wait_recv()


def solution(mesh):
    n_gx = mesh.shape["gx"]
    assert mesh.shape["gy"] == CORES

    def local(snapshot, factor_x, factor_y, factor_var):
        local_x, local_y, n_var, depth = snapshot.shape
        n_q = factor_var.shape[1]
        half_p = factor_y.shape[1]
        rank = factor_x.shape[1]
        k = half_p * n_q // n_gx
        scale = 1.0 / (rank * half_p * CORES * n_q)
        f32 = jnp.float32
        block = (n_gx, local_x, k, depth)
        dma = pltpu.SemaphoreType.DMA
        return pl.pallas_call(
            functools.partial(kernel, n_gx, scale),
            out_shape=jax.ShapeDtypeStruct((depth, depth), f32),
            in_specs=[
                pl.BlockSpec(memory_space=pltpu.HBM),
                pl.BlockSpec(memory_space=pltpu.HBM),
                pl.BlockSpec(memory_space=pltpu.HBM),
                pl.BlockSpec(memory_space=pltpu.HBM),
            ],
            out_specs=pl.BlockSpec(memory_space=pltpu.VMEM),
            scratch_shapes=[
                pltpu.VMEM(factor_x.shape, f32),
                pltpu.VMEM((half_p, local_y * CORES), f32),
                pltpu.SMEM((n_q, n_var), f32),
                pltpu.VMEM((local_x, n_var, local_y, depth), f32),
                pltpu.VMEM((n_q, local_y, local_x * depth), f32),
                pltpu.VMEM((n_gx, local_x, 1, depth), f32),
                pltpu.VMEM((half_p, local_y), f32),
                pltpu.VMEM((half_p, local_y), f32),
                pltpu.VMEM(block, f32),
                pltpu.VMEM(block, f32),
                pltpu.VMEM(block, f32),
                pltpu.VMEM(block, f32),
                pltpu.VMEM((depth, depth), f32),
                pltpu.VMEM((depth // CORES, depth), f32),
                pltpu.VMEM((n_gx, depth // CORES, depth), f32),
                dma((3,)), dma((local_x * CHUNKS,)), dma((2,)),
                dma((n_gx,)), dma((n_gx,)),
                dma((n_q,)), dma((n_q,)),
                dma((n_gx,)), dma((n_gx,)),
                dma((n_gx,)), dma((n_gx,)),
                dma((4,)),
            ],
            compiler_params=pltpu.CompilerParams(
                collective_id=0, has_side_effects=True, vmem_limit_bytes=24 * 1024 * 1024
            ),
        )(*[pltpu.with_memory_space_constraint(a, pltpu.HBM) for a in (jnp.transpose(snapshot, (0, 2, 1, 3)), factor_x, factor_y.T, factor_var.T)])

    in_specs = (P(("snap", "gx"), "gy", None, None), P("gx", None), P(None, "gy"), P())
    return jax.shard_map(local, mesh=mesh, in_specs=in_specs, out_specs=P("snap", None), check_vma=False)
```

time: 27.8 us -> 22.8 us (0.82)
  local copies, waits for them, and re-layouts: 4.24 us -> 0.63 us
  Pallas kernels: 23.3 us -> 22 us
    unnamed x8 -> x1, local copies, waits for them, and re-layouts: 4.24 us -> 0.63 us
    pallas_call x1, Pallas kernels: 23.3 us -> 22 us  [local(): pl.pallas_call(functools.partial(kernel, n_gx, scale), out_shape=jax.Shap...]
where the time goes in v2:
time: 22.8 us; the launch traced here: 22.7 us
  Pallas kernels  22 us (96%)
  local copies, waits for them, and re-layouts  0.63 us (3%)
    pallas_call x1, Pallas kernels, local(): pl.pallas_call(functools.partial(kernel, n_gx, scale), out_shape=jax.Shap...  22 us
    unnamed x1, local copies, waits for them, and re-layouts  0.63 us

profile of v2, /device:TPU:0, one launch (start us, length us, event | category | flops | bytes accessed | tf_op | source)
XLA Modules:
  0.0 22.7 jit_solution(10070179170453700229)
XLA Ops:
  0.0 22.0 %shard_map.46 = f32[128,128]{1,0:T(8,128)S(1)} custom-call(f32[2,12,128,128]{3,2,1,0:T(8,128)} %bitcast.3, f32[2,64]{1,0:T(2,128)} %fx_in.1, f32[32,256]{1,0:T(8,128)} %bitcast.4, f32[4,12]{1,0:T(4,128)} %bitcast.5), custom_call_target="tpu_custom_call" | custom-call | tf_op jit(solution)/shard_map/pallas_call | solution.py:206
  22.0 0.6 %copy.6 = f32[128,128]{1,0:T(8,128)} copy(f32[128,128]{1,0:T(8,128)S(1)} %shard_map.46) | data formatting | bytes 131072

commit v3 on v2

--- a/solution.py
+++ b/solution.py
@@ -17,6 +17,24 @@
     return lax.dot_general(a, b, (dims, ((), ())), precision=HIGHEST, preferred_element_type=jnp.float32)
 
 
+def dot3(a, b, dims=((1,), (0,))):
+    def part(x, y):
+        return lax.dot_general(x, y, (dims, ((), ())), preferred_element_type=jnp.float32)
+
+    a_high, b_high = a.astype(jnp.bfloat16), b.astype(jnp.bfloat16)
+    a_low = (a - a_high.astype(jnp.float32)).astype(jnp.bfloat16)
+    b_low = (b - b_high.astype(jnp.float32)).astype(jnp.bfloat16)
+    return part(a_high, b_high) + (part(a_high, b_low) + part(a_low, b_high))
+
+
+def flip(i, s, n):
+    found, digit = 0, 1
+    while digit < n:
+        found = found + digit * ((i // digit + s // digit) % 2)
+        digit *= 2
+    return found
+
+
 def loop(first, last, body):
     def step(i, carry):
         body(i)
@@ -28,7 +46,7 @@
 def kernel(
     n_gx, scale,
     snap_in, fx_in, fyt_in, fv_in, out_ref,
-    fx_ref, fyt_ref, fv_ref, snap, reduced, fx_all, fy_send, fy_recv, half_send, half_recv, part, blocks, gram, gram_recv, pieces,
+    fx_ref, fyt_ref, fv_ref, snap, reduced, fx_all, fy_recv, half_send, half_recv, part, blocks, gram, gram_recv, pieces, summed,
     in_sems, snap_sem, fy_sems, fx_send, fx_recv, half_ssem, half_rsem, a2a_send, a2a_recv, rs_send, rs_recv, core_sems,
 ):
     gx, gy = lax.axis_index("gx"), lax.axis_index("gy")
@@ -37,7 +55,7 @@
     n_q = reduced.shape[0]
     _, _, k, _ = blocks.shape
     per_q = n_gx // n_q
-    half_rows = depth // CORES
+    half_rows = depth * 5 // 8 // CORES
 
     def remote(src, dst, send, recv, where):
         return pltpu.make_async_remote_copy(
@@ -64,6 +82,10 @@
     loop(1, n_gx, lambda s: pl.semaphore_signal(
         barrier, inc=1, device_id={"gx": lax.rem(gx + s, n_gx)}, device_id_type=MESH))
 
+    pl.semaphore_wait(barrier, n_gx)
+    other_y = pl.ds(pl.multiple_of(other * local_y, local_y), local_y)
+    fy_copy = remote(fyt_in.at[:, other_y], fy_recv, fy_sems.at[0], fy_sems.at[1], {"gy": other})
+    fy_copy.start()
     for load in small:
         load.wait()
     fx = fx_ref[...]
@@ -71,13 +93,7 @@
     fx_wide = jnp.concatenate([fx, jnp.zeros((local_x, depth - rank), jnp.float32)], axis=1) if rank < depth else fx
     for x in range(local_x):
         fx_all[gx, x] = fx_wide[x : x + 1]
-    fy_send[...] = fyt_ref[:, pl.ds(pl.multiple_of(other * local_y, local_y), local_y)]
     fy_mine = fyt_ref[:, pl.ds(pl.multiple_of(gy * local_y, local_y), local_y)]
-
-    pl.semaphore_wait(barrier, n_gx)
-
-    fy_copy = remote(fy_send, fy_recv, fy_sems.at[0], fy_sems.at[1], {"gy": other})
-    fy_copy.start()
 
     def fx_copy(j):
         return remote(fx_all.at[gx], fx_all.at[gx], fx_send.at[j], fx_recv.at[gx], {"gx": j})
@@ -106,26 +122,27 @@
     def put(ref, q, value):
         for x in range(local_x):
             cells = value[:, x * depth : (x + 1) * depth]
-            ref[q * per_q : (q + 1) * per_q, x] = cells.reshape(per_q, k, depth)
+            ref[pl.ds(q * per_q, per_q), x] = cells.reshape(per_q, k, depth)
 
     fy_copy.wait_recv()
     fy_theirs = fy_recv[...]
     halves = []
-    for q in range(n_q):
-        put(half_send, q, dot(fy_theirs, reduced[q]))
+    order = range(n_q)
+    for q in order:
+        put(half_send, q, dot3(fy_theirs, reduced[q]))
         at = pl.ds(q * per_q, per_q)
         exchange = remote(half_send.at[at], half_recv.at[at], half_ssem.at[q], half_rsem.at[q], {"gy": other})
         exchange.start()
         halves.append(exchange)
-    for q in range(n_q):
-        put(part, q, dot(fy_mine, reduced[q]))
+    for q in order:
+        put(part, q, dot3(fy_mine, reduced[q]))
 
     def block_copy(j):
         return remote(part.at[j], blocks.at[gx], a2a_send.at[j], a2a_recv.at[gx], {"gx": j})
 
-    for q in range(n_q):
+    for q, exchange in zip(order, halves):
         at = pl.ds(q * per_q, per_q)
-        halves[q].wait_recv()
+        exchange.wait_recv()
         part[at] = part[at] + half_recv[at]
 
         def send_block(j):
@@ -133,7 +150,7 @@
             def _():
                 block_copy(j).start()
 
-        loop(q * per_q, (q + 1) * per_q, send_block)
+        loop(0, per_q, lambda i, q=q: send_block(q * per_q + i))
     blocks[gx] = part[gx]
 
     def arrived(sems, ref, j):
@@ -153,10 +170,16 @@
 
     loop(1, n_gx, lambda s: arrived(a2a_recv, blocks, lax.rem(gx + s, n_gx)))
     cells = blocks[...].reshape(wide, depth) * largest
-    gram[...] = dot(cells, dot(mixing, cells), ((0,), (0,)))
+    square = dot3(cells, dot3(mixing, cells), ((0,), (0,)))
+    side = depth // 4
+    lane = lax.broadcasted_iota(jnp.int32, (side, depth), 1)
+    gram[:side] = square[:side]
+    gram[side : 2 * side] = jnp.where(lane < side, pltpu.roll(square[3 * side :], side, 1), square[side : 2 * side])
+    third, split = square[2 * side : 3 * side], side // 2
+    gram[2 * side :] = jnp.where(lane[:split] < 2 * side, pltpu.roll(third[split:], 2 * side, 1), third[:split])
 
     def others(body):
-        loop(1, n_gx, lambda s: body(lax.rem(gx + s, n_gx)))
+        loop(1, n_gx, lambda s: body(flip(gx, s, n_gx)))
 
     my_rows = pl.ds(pl.multiple_of(gy * half_rows, half_rows), half_rows)
     other_rows = pl.ds(pl.multiple_of(other * half_rows, half_rows), half_rows)
@@ -170,8 +193,8 @@
 
     others(lambda t: piece_copy(t).start())
     others(lambda t: remote(pieces.at[gx], pieces.at[t], rs_send.at[t], rs_recv.at[t], {"gx": t}).wait_recv())
-    out_ref[my_rows] = jnp.sum(pieces[...], axis=0) * scale
-    out_copy = remote(out_ref.at[my_rows], out_ref.at[my_rows], core_sems.at[2], core_sems.at[3], {"gy": other})
+    summed[my_rows] = jnp.sum(pieces[...], axis=0) * scale
+    out_copy = remote(summed.at[my_rows], summed.at[my_rows], core_sems.at[2], core_sems.at[3], {"gy": other})
     out_copy.start()
 
     fy_copy.wait_send()
@@ -185,8 +208,15 @@
     loop(1, n_gx, lambda s: sent(lax.rem(gx + s, n_gx)))
     others(lambda t: piece_copy(t).wait_send())
     gram_copy.wait_send()
+    remote(summed.at[my_rows], summed.at[other_rows], core_sems.at[2], core_sems.at[3], {"gy": other}).wait_recv()
+    third = summed[2 * side :]
+    upper = jnp.concatenate([
+        summed[: 2 * side], third, pltpu.roll(third, 2 * side, 1), pltpu.roll(summed[side : 2 * side], depth - side, 1)
+    ], axis=0)
+    row_block = lax.broadcasted_iota(jnp.int32, (depth, depth), 0) // side
+    lane_block = lax.broadcasted_iota(jnp.int32, (depth, depth), 1) // side
+    out_ref[...] = jnp.where(row_block > lane_block, upper.T, upper)
     out_copy.wait_send()
-    remote(out_ref.at[my_rows], out_ref.at[other_rows], core_sems.at[2], core_sems.at[3], {"gy": other}).wait_recv()
 
 
 def solution(mesh):
@@ -202,6 +232,7 @@
         scale = 1.0 / (rank * half_p * CORES * n_q)
         f32 = jnp.float32
         block = (n_gx, local_x, k, depth)
+        packed = depth * 5 // 8
         dma = pltpu.SemaphoreType.DMA
         return pl.pallas_call(
             functools.partial(kernel, n_gx, scale),
@@ -221,14 +252,14 @@
                 pltpu.VMEM((n_q, local_y, local_x * depth), f32),
                 pltpu.VMEM((n_gx, local_x, 1, depth), f32),
                 pltpu.VMEM((half_p, local_y), f32),
-                pltpu.VMEM((half_p, local_y), f32),
-                pltpu.VMEM(block, f32),
-                pltpu.VMEM(block, f32),
-                pltpu.VMEM(block, f32),
-                pltpu.VMEM(block, f32),
-                pltpu.VMEM((depth, depth), f32),
-                pltpu.VMEM((depth // CORES, depth), f32),
-                pltpu.VMEM((n_gx, depth // CORES, depth), f32),
+                pltpu.VMEM(block, f32),
+                pltpu.VMEM(block, f32),
+                pltpu.VMEM(block, f32),
+                pltpu.VMEM(block, f32),
+                pltpu.VMEM((packed, depth), f32),
+                pltpu.VMEM((packed // CORES, depth), f32),
+                pltpu.VMEM((n_gx, packed // CORES, depth), f32),
+                pltpu.VMEM((packed, depth), f32),
                 dma((3,)), dma((local_x * CHUNKS,)), dma((2,)),
                 dma((n_gx,)), dma((n_gx,)),
                 dma((n_q,)), dma((n_q,)),

time: 22.8 us -> 23 us (level)
  Pallas kernels: 22 us -> 22.3 us
where the time goes in v3:
time: 23 us; the launch traced here: 22.9 us
  Pallas kernels  22.3 us (97%)
  local copies, waits for them, and re-layouts  0.63 us (3%)
    pallas_call x1, Pallas kernels, local(): pl.pallas_call(functools.partial(kernel, n_gx, scale), out_shape=jax.Shap...  22.3 us
    unnamed x1, local copies, waits for them, and re-layouts  0.63 us

profile of v3, /device:TPU:0, one launch (start us, length us, event | category | flops | bytes accessed | tf_op | source)
XLA Modules:
  0.0 22.9 jit_solution(7450829300720595525)
XLA Ops:
  0.0 22.3 %shard_map.46 = f32[128,128]{1,0:T(8,128)S(1)} custom-call(f32[2,12,128,128]{3,2,1,0:T(8,128)} %bitcast.3, f32[2,64]{1,0:T(2,128)} %fx_in.1, f32[32,256]{1,0:T(8,128)} %bitcast.4, f32[4,12]{1,0:T(4,128)} %bitcast.5), custom_call_target="tpu_custom_call" | custom-call | tf_op jit(solution)/shard_map/pallas_call | solution.py:237
  22.3 0.6 %copy.6 = f32[128,128]{1,0:T(8,128)} copy(f32[128,128]{1,0:T(8,128)S(1)} %shard_map.46) | data formatting | bytes 131072

commit v4 on v3

--- a/solution.py
+++ b/solution.py
@@ -25,14 +25,6 @@
     a_low = (a - a_high.astype(jnp.float32)).astype(jnp.bfloat16)
     b_low = (b - b_high.astype(jnp.float32)).astype(jnp.bfloat16)
     return part(a_high, b_high) + (part(a_high, b_low) + part(a_low, b_high))
-
-
-def flip(i, s, n):
-    found, digit = 0, 1
-    while digit < n:
-        found = found + digit * ((i // digit + s // digit) % 2)
-        digit *= 2
-    return found
 
 
 def loop(first, last, body):
@@ -127,20 +119,19 @@
     fy_copy.wait_recv()
     fy_theirs = fy_recv[...]
     halves = []
-    order = range(n_q)
-    for q in order:
+    for q in range(n_q):
         put(half_send, q, dot3(fy_theirs, reduced[q]))
         at = pl.ds(q * per_q, per_q)
         exchange = remote(half_send.at[at], half_recv.at[at], half_ssem.at[q], half_rsem.at[q], {"gy": other})
         exchange.start()
         halves.append(exchange)
-    for q in order:
+    for q in range(n_q):
         put(part, q, dot3(fy_mine, reduced[q]))
 
     def block_copy(j):
         return remote(part.at[j], blocks.at[gx], a2a_send.at[j], a2a_recv.at[gx], {"gx": j})
 
-    for q, exchange in zip(order, halves):
+    for q, exchange in enumerate(halves):
         at = pl.ds(q * per_q, per_q)
         exchange.wait_recv()
         part[at] = part[at] + half_recv[at]
@@ -179,7 +170,7 @@
     gram[2 * side :] = jnp.where(lane[:split] < 2 * side, pltpu.roll(third[split:], 2 * side, 1), third[:split])
 
     def others(body):
-        loop(1, n_gx, lambda s: body(flip(gx, s, n_gx)))
+        loop(1, n_gx, lambda s: body(lax.rem(gx + s, n_gx)))
 
     my_rows = pl.ds(pl.multiple_of(gy * half_rows, half_rows), half_rows)
     other_rows = pl.ds(pl.multiple_of(other * half_rows, half_rows), half_rows)

time: 23 us -> 21.3 us (0.926)
  Pallas kernels: 22.3 us -> 20.6 us
    pallas_call x1, Pallas kernels: 22.3 us -> 20.6 us  [local(): pl.pallas_call(functools.partial(kernel, n_gx, scale), out_shape=jax.Shap...]
where the time goes in v4:
time: 21.3 us; the launch traced here: 21.2 us
  Pallas kernels  20.6 us (97%)
  local copies, waits for them, and re-layouts  0.63 us (3%)
    pallas_call x1, Pallas kernels, local(): pl.pallas_call(functools.partial(kernel, n_gx, scale), out_shape=jax.Shap...  20.6 us
    unnamed x1, local copies, waits for them, and re-layouts  0.63 us

profile of v4, /device:TPU:0, one launch (start us, length us, event | category | flops | bytes accessed | tf_op | source)
XLA Modules:
  0.0 21.2 jit_solution(14777026088123693710)
XLA Ops:
  0.0 20.6 %shard_map.46 = f32[128,128]{1,0:T(8,128)S(1)} custom-call(f32[2,12,128,128]{3,2,1,0:T(8,128)} %bitcast.3, f32[2,64]{1,0:T(2,128)} %fx_in.1, f32[32,256]{1,0:T(8,128)} %bitcast.4, f32[4,12]{1,0:T(4,128)} %bitcast.5), custom_call_target="tpu_custom_call" | custom-call | tf_op jit(solution)/shard_map/pallas_call | solution.py:228
  20.6 0.6 %copy.6 = f32[128,128]{1,0:T(8,128)} copy(f32[128,128]{1,0:T(8,128)S(1)} %shard_map.46) | data formatting | bytes 131072

commit v5 on v4

--- a/solution.py
+++ b/solution.py
@@ -92,7 +92,7 @@
 
     loop(1, n_gx, lambda s: fx_copy(lax.rem(gx + s, n_gx)).start())
 
-    rows = 16
+    rows = 32
     for part_of, load in enumerate(loads):
         x, first = part_of // CHUNKS, part_of % CHUNKS * chunk
         load.wait()
@@ -117,16 +117,17 @@
             ref[pl.ds(q * per_q, per_q), x] = cells.reshape(per_q, k, depth)
 
     fy_copy.wait_recv()
-    fy_theirs = fy_recv[...]
+    fy_both = jnp.concatenate([fy_recv[...], fy_mine], axis=0)
+    half_p = fy_recv.shape[0]
     halves = []
     for q in range(n_q):
-        put(half_send, q, dot3(fy_theirs, reduced[q]))
+        both = dot(fy_both, reduced[q])
+        put(half_send, q, both[:half_p])
+        put(part, q, both[half_p:])
         at = pl.ds(q * per_q, per_q)
         exchange = remote(half_send.at[at], half_recv.at[at], half_ssem.at[q], half_rsem.at[q], {"gy": other})
         exchange.start()
         halves.append(exchange)
-    for q in range(n_q):
-        put(part, q, dot3(fy_mine, reduced[q]))
 
     def block_copy(j):
         return remote(part.at[j], blocks.at[gx], a2a_send.at[j], a2a_recv.at[gx], {"gx": j})

time: 21.3 us -> 21.2 us (level)
  no operation moved by 1% of the time
where the time goes in v5:
time: 21.2 us; the launch traced here: 21.1 us
  Pallas kernels  20.4 us (96%)
  local copies, waits for them, and re-layouts  0.63 us (3%)
    pallas_call x1, Pallas kernels, local(): pl.pallas_call(functools.partial(kernel, n_gx, scale), out_shape=jax.Shap...  20.4 us
    unnamed x1, local copies, waits for them, and re-layouts  0.63 us

profile of v5, /device:TPU:0, one launch (start us, length us, event | category | flops | bytes accessed | tf_op | source)
XLA Modules:
  0.0 21.1 jit_solution(15228742502494437607)
XLA Ops:
  0.0 20.4 %shard_map.46 = f32[128,128]{1,0:T(8,128)S(1)} custom-call(f32[2,12,128,128]{3,2,1,0:T(8,128)} %bitcast.3, f32[2,64]{1,0:T(2,128)} %fx_in.1, f32[32,256]{1,0:T(8,128)} %bitcast.4, f32[4,12]{1,0:T(4,128)} %bitcast.5), custom_call_target="tpu_custom_call" | custom-call | tf_op jit(solution)/shard_map/pallas_call | solution.py:229
  20.4 0.6 %copy.6 = f32[128,128]{1,0:T(8,128)} copy(f32[128,128]{1,0:T(8,128)S(1)} %shard_map.46) | data formatting | bytes 131072

commit v6 on v5

--- a/solution.py
+++ b/solution.py
@@ -39,7 +39,7 @@
     n_gx, scale,
     snap_in, fx_in, fyt_in, fv_in, out_ref,
     fx_ref, fyt_ref, fv_ref, snap, reduced, fx_all, fy_recv, half_send, half_recv, part, blocks, gram, gram_recv, pieces, summed,
-    in_sems, snap_sem, fy_sems, fx_send, fx_recv, half_ssem, half_rsem, a2a_send, a2a_recv, rs_send, rs_recv, core_sems,
+    in_sems, snap_sem, fy_sems, fx_send, fx_recv, half_ssem, half_rsem, a2a_send, a2a_recv, rs_send, rs_recv, core_sems, gram_sems,
 ):
     gx, gy = lax.axis_index("gx"), lax.axis_index("gy")
     other = 1 - gy
@@ -173,18 +173,29 @@
     def others(body):
         loop(1, n_gx, lambda s: body(lax.rem(gx + s, n_gx)))
 
-    my_rows = pl.ds(pl.multiple_of(gy * half_rows, half_rows), half_rows)
-    other_rows = pl.ds(pl.multiple_of(other * half_rows, half_rows), half_rows)
-    gram_copy = remote(gram.at[other_rows], gram_recv, core_sems.at[0], core_sems.at[1], {"gy": other})
-    gram_copy.start()
-    gram_copy.wait_recv()
-    pieces[gx] = gram[my_rows] + gram_recv[...]
-
-    def piece_copy(t):
-        return remote(pieces.at[gx], pieces.at[gx], rs_send.at[t], rs_recv.at[gx], {"gx": t})
-
-    others(lambda t: piece_copy(t).start())
-    others(lambda t: remote(pieces.at[gx], pieces.at[t], rs_send.at[t], rs_recv.at[t], {"gx": t}).wait_recv())
+    my_rows = pl.ds(pl.multiple_of(gy * half_rows, 8), half_rows)
+    other_rows = pl.ds(pl.multiple_of(other * half_rows, 8), half_rows)
+    first = half_rows // 16 * 8
+    spans = ((0, first), (first, half_rows - first))
+
+    def gram_copy(i):
+        at, size = spans[i]
+        theirs = pl.ds(pl.multiple_of(other * half_rows + at, 8), size)
+        return remote(gram.at[theirs], gram_recv.at[pl.ds(at, size)], gram_sems.at[i], gram_sems.at[2 + i], {"gy": other})
+
+    def piece_copy(i, t, source):
+        at = pl.ds(*spans[i])
+        return remote(pieces.at[gx, at], pieces.at[source, at], rs_send.at[i, t], rs_recv.at[i, source], {"gx": t})
+
+    for i in range(2):
+        gram_copy(i).start()
+    for i, (at, size) in enumerate(spans):
+        gram_copy(i).wait_recv()
+        mine = pl.ds(pl.multiple_of(gy * half_rows + at, 8), size)
+        pieces[gx, pl.ds(at, size)] = gram[mine] + gram_recv[pl.ds(at, size)]
+        others(lambda t, i=i: piece_copy(i, t, gx).start())
+    for i in range(2):
+        others(lambda t, i=i: piece_copy(i, t, t).wait_recv())
     summed[my_rows] = jnp.sum(pieces[...], axis=0) * scale
     out_copy = remote(summed.at[my_rows], summed.at[my_rows], core_sems.at[2], core_sems.at[3], {"gy": other})
     out_copy.start()
@@ -198,8 +209,9 @@
         block_copy(j).wait_send()
 
     loop(1, n_gx, lambda s: sent(lax.rem(gx + s, n_gx)))
-    others(lambda t: piece_copy(t).wait_send())
-    gram_copy.wait_send()
+    for i in range(2):
+        others(lambda t, i=i: piece_copy(i, t, gx).wait_send())
+        gram_copy(i).wait_send()
     remote(summed.at[my_rows], summed.at[other_rows], core_sems.at[2], core_sems.at[3], {"gy": other}).wait_recv()
     third = summed[2 * side :]
     upper = jnp.concatenate([
@@ -256,8 +268,8 @@
                 dma((n_gx,)), dma((n_gx,)),
                 dma((n_q,)), dma((n_q,)),
                 dma((n_gx,)), dma((n_gx,)),
-                dma((n_gx,)), dma((n_gx,)),
-                dma((4,)),
+                dma((2, n_gx)), dma((2, n_gx)),
+                dma((4,)), dma((4,)),
             ],
             compiler_params=pltpu.CompilerParams(
                 collective_id=0, has_side_effects=True, vmem_limit_bytes=24 * 1024 * 1024

time: 21.2 us -> 22.1 us (1.042)
  Pallas kernels: 20.4 us -> 21.4 us
    pallas_call x1, Pallas kernels: 20.4 us -> 21.4 us  [local(): pl.pallas_call(functools.partial(kernel, n_gx, scale), out_shape=jax.Shap...]
where the time goes in v6:
time: 22.1 us; the launch traced here: 22 us
  Pallas kernels  21.4 us (97%)
  local copies, waits for them, and re-layouts  0.63 us (3%)
    pallas_call x1, Pallas kernels, local(): pl.pallas_call(functools.partial(kernel, n_gx, scale), out_shape=jax.Shap...  21.4 us
    unnamed x1, local copies, waits for them, and re-layouts  0.63 us

profile of v6, /device:TPU:0, one launch (start us, length us, event | category | flops | bytes accessed | tf_op | source)
XLA Modules:
  0.0 22.0 jit_solution(10635228499668172348)
XLA Ops:
  0.0 21.4 %shard_map.46 = f32[128,128]{1,0:T(8,128)S(1)} custom-call(f32[2,12,128,128]{3,2,1,0:T(8,128)} %bitcast.3, f32[2,64]{1,0:T(2,128)} %fx_in.1, f32[32,256]{1,0:T(8,128)} %bitcast.4, f32[4,12]{1,0:T(4,128)} %bitcast.5), custom_call_target="tpu_custom_call" | custom-call | tf_op jit(solution)/shard_map/pallas_call | solution.py:241
  21.4 0.6 %copy.6 = f32[128,128]{1,0:T(8,128)} copy(f32[128,128]{1,0:T(8,128)S(1)} %shard_map.46) | data formatting | bytes 131072
